TPU v7x, 512 devices: a whole 4x4x16 slice. The times are simulated.
512 devices in a mesh: aux: 64 (over x, z), pair: 8 (over y, core).
Axes of the slice: x: 4, y: 4, z: 16, core: 2. Of those that a mesh axis runs over, the one named last changes fastest.
Arguments:
- three_center: bfloat16 [512, 64, 1024], P('aux', 'pair'), may hold values from -6 to 6
- tile_live: int32 [64, 64], P('aux', 'pair'), may hold values from 0 to 1
- pair_atoms: int32 [64], replicated, may hold values from 0 to 63, each once
- green_occ: bfloat16 [256, 256], replicated, may hold values from -0.375 to 0.375
- green_vir: bfloat16 [256, 256], replicated, may hold values from -0.375 to 0.375
- screened: bfloat16 [512, 40], P('aux'), may hold values from -1 to 1
Outputs:
- polarizability: float32 [512, 40], P('aux', 'pair')
- self_energy: float32 [64, 1024], P('pair')
Inputs may be any that keep to these rules, and one draw needn't show every extreme that they name: `pair_atoms`: a permutation of the 64 atom pairs.
All inputs are finite; a program needn't handle non-finite values.
Results may differ from a plain program's by a relative error of at most 0.0043.
Values may be sent and summed in bfloat16 or wider, within the bound.
A program may use at most 64 MiB of HBM per device.

v0:
```python
import math
import jax
import jax.numpy as jnp
from jax import lax
from jax.sharding import PartitionSpec as P

OA = 32
NAT = 8
REACH = 2


def shifted(value, axis, steps):
    count = lax.axis_size(axis)
    initial, last = (max(0, -steps), min(count, count - steps))
    return lax.ppermute(value, axis, [(source, source + steps) for source in range(initial, last)])


def side_by_side(arrays, axis, split_dim, concat_dim, along):
    ends, at = ([], 0)
    for a in arrays[:-1]:
        at += a.shape[along]
        ends.append(at)
    both = jnp.concatenate(arrays, axis=along)
    return tuple(
        jnp.split(
            lax.all_to_all(both, axis, split_axis=split_dim, concat_axis=concat_dim, tiled=True),
            ends,
            axis=along,
        )
    )


def in_blocks(array, dim, peers):
    before, after = (array.shape[:dim], array.shape[dim + 1 :])
    return jnp.moveaxis(array.reshape(*before, peers, -1, *after), dim, 0)


def summed_on_arrival(array, axis, dim):
    peers = lax.axis_size(axis)
    blocks = lax.all_to_all(in_blocks(array, dim, peers), axis, 0, 0, tiled=True)
    return jnp.sum(blocks, axis=0)


def from_everyone(array, axis):
    peers = lax.axis_size(axis)
    return lax.all_to_all(
        jnp.broadcast_to(array[None], (peers, *array.shape)), axis, 0, 0, tiled=True
    )


def joined_along(blocks, dim):
    shape = list(blocks.shape[1:])
    shape[dim] *= blocks.shape[0]
    return jnp.moveaxis(blocks, 0, dim).reshape(shape)


def gather_directly(array, axis, dim):
    blocks = from_everyone(array, axis)
    return joined_along(blocks, dim)


def tiles_to_matrix(tile_data, inverse):
    tile_rows = tile_data.shape[0]
    ordered = jnp.take(tile_data, inverse, axis=1)
    reshaped = ordered.reshape(tile_rows, NAT, NAT, OA, OA)
    return jnp.transpose(reshaped, (0, 1, 3, 2, 4)).reshape(tile_rows, NAT * OA, NAT * OA)


def matrix_to_tiles(matrix, pair_atoms):
    tile_rows = matrix.shape[0]
    reshaped = matrix.reshape(tile_rows, NAT, OA, NAT, OA)
    ordered = jnp.transpose(reshaped, (0, 1, 3, 2, 4)).reshape(tile_rows, NAT * NAT, OA * OA)
    return jnp.take(ordered, pair_atoms, axis=1)


def neighbor_window(masked):
    pieces = []
    for offset in range(-REACH, REACH + 1):
        if offset == 0:
            pieces.append(masked)
        else:
            pieces.append(shifted(masked, "aux", -offset))
    return jnp.concatenate(pieces, axis=0)


def row_groups(orbital_form, group_fn):
    row_count = orbital_form.shape[0]
    group_size = math.gcd(row_count, 8)
    grouped = orbital_form.reshape(row_count // group_size, group_size, NAT * OA, NAT * OA)
    result = lax.map(group_fn, grouped)
    return result.reshape((row_count,) + result.shape[2:])


def all_products(orbital_form, green_occ, green_vir):

    def group_fn(row_group):
        left_half = jnp.einsum(
            "lu,plm->pum", green_occ, row_group, preferred_element_type=jnp.float32
        ).astype(jnp.bfloat16)
        return jnp.einsum(
            "pum,mv->puv", left_half, green_vir, preferred_element_type=jnp.float32
        ).astype(jnp.bfloat16)

    return row_groups(orbital_form, group_fn)


def energy_rows(mixed_tiles, occ_rows, orbital_form, tile_first):
    tile_rows, tile_count = (mixed_tiles.shape[0], mixed_tiles.shape[1])
    mixed_tiles = mixed_tiles.reshape(tile_rows, tile_count, OA, OA)
    scaled_rows = jnp.einsum(
        "qkml,kls->qkms", mixed_tiles, occ_rows, preferred_element_type=jnp.float32
    ).astype(jnp.bfloat16)
    term_sums = jnp.einsum(
        "qkms,qsn->kmn", scaled_rows, orbital_form, preferred_element_type=jnp.float32
    )
    atom_onehot = (tile_first[:, None] == jnp.arange(NAT, dtype=jnp.int32)[None, :]).astype(
        jnp.float32
    )
    return jnp.einsum("ka,kmn->amn", atom_onehot, term_sums, precision=lax.Precision.HIGHEST)


def per_device(three_center, tile_live, pair_atoms, green_occ, green_vir, screened):
    row_count, own_count = (three_center.shape[0], three_center.shape[1])
    masked = three_center * tile_live[0].astype(jnp.bfloat16)[:, None]
    inverse = jnp.argsort(pair_atoms)
    first_atom = pair_atoms // NAT
    second_atom = pair_atoms % NAT
    occ_rows = green_occ.reshape(NAT, OA, NAT * OA)
    window = neighbor_window(masked)
    flat_window = window.reshape(window.shape[0], own_count * OA * OA)
    mixed_tiles = jnp.dot(screened, flat_window, preferred_element_type=jnp.float32).astype(
        jnp.bfloat16
    )
    mixed_tiles = mixed_tiles.reshape(row_count, own_count, OA * OA)
    sub_tiles, sub_mixed = side_by_side((masked, mixed_tiles), "pair", 0, 1, 2)
    orbital_form = tiles_to_matrix(sub_tiles, inverse)
    full_form = all_products(orbital_form, green_occ, green_vir)
    products = lax.all_to_all(
        matrix_to_tiles(full_form, pair_atoms), "pair", split_axis=1, concat_axis=0, tiled=True
    )
    by_atom = energy_rows(
        sub_mixed, jnp.take(occ_rows, second_atom, axis=0), orbital_form, first_atom
    )
    chi_part = lax.dot_general(
        products.reshape(row_count, own_count * OA * OA),
        flat_window,
        (((1,), (1,)), ((), ())),
        preferred_element_type=jnp.float32,
    ) * (1.0 / (OA * NAT))
    polarizability = summed_on_arrival(chi_part, "pair", 1)
    aux_total = row_count * lax.axis_size("aux")
    sigma_scale = 1.0 / math.sqrt(aux_total * NAT * OA * NAT)
    partial_value = (
        matrix_to_tiles(by_atom.reshape(1, NAT * OA, NAT * OA), pair_atoms)[0] * -sigma_scale
    )
    columns = summed_on_arrival(partial_value, "aux", 1)
    owned_tiles = summed_on_arrival(columns, "pair", 0)
    self_energy = gather_directly(owned_tiles, "aux", 1)
    return (polarizability, self_energy)


def solution(mesh):
    placed = (P("aux", "pair", None), P("aux", "pair"), P(), P(), P(), P("aux", None))
    return jax.shard_map(
        per_device,
        mesh=mesh,
        in_specs=placed,
        out_specs=(P("aux", "pair"), P("pair", None)),
        check_vma=False,
    )
```

profile of v0, /device:TPU:1, one launch (start us, length us, event | category | flops | bytes accessed | tf_op | source)
XLA Modules:
  0.0 136.3 jit_solution(14606263857130700433)
XLA Ops:
  0.7 0.7 convert_bitcast_fusion
  1.4 1.0 broadcast_multiply_fusion
  2.3 5.7 %collective-permute-start = (bf16[8,8,1024]{2,1,0:T(8,128)(2,1)S(1)}, bf16[8,8,1024]{2,1,0:T(8,128)(2,1)S(1)}, u32[]{:S(2)}, u32[]{:S(2)}) collective-permute-start(bf16[8,8,1024]{2,1,0:T(8,128)(2,1)S(1)} %broadcast_multiply_fusion), channel_id=1, source_target_pairs={{0,16},{8,24},{16,32},{24,40},{32,48},{40,56},{48,64},{56,72},{64,... | collective-permute-start | bytes 393224 | tf_op jit(solution)/shard_map/ppermute | solution.py:15
  8.1 3.5 %collective-permute-start.1 = (bf16[8,8,1024]{2,1,0:T(8,128)(2,1)S(1)}, bf16[8,8,1024]{2,1,0:T(8,128)(2,1)S(1)}, u32[]{:S(2)}, u32[]{:S(2)}) collective-permute-start(bf16[8,8,1024]{2,1,0:T(8,128)(2,1)S(1)} %broadcast_multiply_fusion), channel_id=1, source_target_pairs={{0,8},{8,16},{16,24},{24,32},{32,40},{40,48},{48,56},{56,64},{64,7... | collective-permute-start | bytes 393224 | tf_op jit(solution)/shard_map/ppermute | solution.py:15
  11.6 1.3 collective-permute-start.2
  12.9 1.3 collective-permute-start.3
  14.2 0.7 compare_and_fusion.2
  14.9 0.7 and_select_fusion.1
  15.6 2.7 %sort.17 = (s32[64]{0:T(128)}, s32[64]{0:T(128)S(1)}) sort(s32[64]{0:T(128)} %param.10, s32[64]{0:T(128)S(1)} %iota.8), dimensions={0}, to_apply=%region_0.0 | sort | flops 384 | bytes 1024 | tf_op jit(solution)/shard_map/jit(argsort)/sort | solution.py:125
  18.3 1.0 constant_dynamic-update-slice_fusion.2
  19.4 6.0 %collective-permute-done.3 = bf16[8,8,1024]{2,1,0:T(8,128)(2,1)S(1)} collective-permute-done((bf16[8,8,1024]{2,1,0:T(8,128)(2,1)S(1)}, bf16[8,8,1024]{2,1,0:T(8,128)(2,1)S(1)}, u32[]{:S(2)}, u32[]{:S(2)}) %collective-permute-start.3) | collective-permute-done | bytes 131104 | tf_op jit(solution)/shard_map/ppermute | solution.py:15
  25.4 0.4 copy.41
  25.8 0.2 convolution_convert_fusion
  26.1 0.7 pad_maximum_fusion
  26.8 7.0 %all-to-all-start = ((bf16[8,8,2048]{2,1,0:T(8,128)(2,1)}), bf16[8,8,2048]{2,1,0:T(8,128)(2,1)S(1)}, u32[]{:S(2)}, u32[]{:S(2)}) async-start(bf16[8,8,2048]{2,1,0:T(8,128)(2,1)} %pad_maximum_fusion), calls=%async_computation | async-start | bytes 524288 | tf_op jit(solution)/shard_map/all_to_all | solution.py:26
  33.8 0.6 gather_fusion
  34.4 5.8 %all-to-all-done = bf16[8,8,2048]{2,1,0:T(8,128)(2,1)S(1)} async-done(((bf16[8,8,2048]{2,1,0:T(8,128)(2,1)}), bf16[8,8,2048]{2,1,0:T(8,128)(2,1)S(1)}, u32[]{:S(2)}, u32[]{:S(2)}) %all-to-all-start) | async-done | bytes 262176 | tf_op jit(solution)/shard_map/all_to_all | solution.py:26
  40.3 0.7 gather_fusion.2
  41.1 0.4 reshape.130
  41.5 0.2 copy.46
  41.7 0.3 reshape.131
  42.1 0.4 reshape.194
  42.4 0.5 convolution_convert_fusion.2
  42.9 0.2 reshape_reshape.7
  43.2 0.5 reshape.190
  43.8 0.7 gather_fusion.3
  44.6 0.2 copy.47
  44.8 0.5 broadcast.66
  45.3 1.4 %reduce.2 = bf16[64,1024]{1,0:T(8,128)(2,1)S(1)} reduce(bf16[64,1,1024]{2,1,0:T(2,128)(2,1)S(1)} %bitcast.84, bf16[]{:T(256)} %broadcast.66), dimensions={1}, to_apply=%bitcast.74.reduce_sub_computation | reduce | bytes 262146
  46.7 0.7 reshape.199
  47.4 4.3 %all-to-all-start.1 = ((bf16[8,2,4096]{2,1,0:T(2,128)(2,1)}), bf16[8,2,4096]{2,1,0:T(2,128)(2,1)S(1)}, u32[]{:S(2)}, u32[]{:S(2)}) async-start(bf16[8,2,4096]{2,1,0:T(2,128)(2,1)} %reshape.199), calls=%async_computation.1 | async-start | bytes 262144 | tf_op jit(solution)/shard_map/all_to_all | solution.py:138
  51.7 0.2 copy.34
  51.9 0.8 copy.35
  52.7 0.5 fusion
  53.2 1.3 fusion.2
  54.5 0.8 fusion.8
  55.2 0.3 reshape_reshape.8
  55.5 0.6 copy.37
  56.1 0.5 reshape.170
  56.6 0.7 gather_fusion.1
  57.3 0.2 copy.38
  57.6 1.0 reshape.201
  58.6 14.4 %all-to-all-start.3 = ((f32[64,1,1024]{2,1,0:T(1,128)}), f32[64,1,1024]{2,1,0:T(1,128)S(1)}, u32[]{:S(2)}, u32[]{:S(2)}) async-start(f32[64,1,1024]{2,1,0:T(1,128)} %reshape.201), calls=%async_computation.3 | async-start | bytes 524288 | tf_op jit(solution)/shard_map/all_to_all | solution.py:40
  73.0 0.1 reshape.200
  73.2 0.7 bitcast_reduce_fusion.1
  74.0 19.1 %all-to-all-done.3 = f32[64,1,1024]{2,1,0:T(1,128)S(1)} async-done(((f32[64,1,1024]{2,1,0:T(1,128)}), f32[64,1,1024]{2,1,0:T(1,128)S(1)}, u32[]{:S(2)}, u32[]{:S(2)}) %all-to-all-start.3) | async-done | bytes 262176 | tf_op jit(solution)/shard_map/all_to_all | solution.py:40
  93.0 0.5 broadcast.67
  93.6 1.3 reduce.3
  94.8 0.1 reshape.202
  95.1 0.7 reshape.203
  95.8 6.2 %all-to-all-start.4 = ((f32[8,1,128]{2,1,0:T(1,128)}), f32[8,1,128]{2,1,0:T(1,128)S(1)}, u32[]{:S(2)}, u32[]{:S(2)}) async-start(f32[8,1,128]{2,1,0:T(1,128)} %reshape.203), calls=%async_computation.4 | async-start | bytes 8192 | tf_op jit(solution)/shard_map/all_to_all | solution.py:40
  102.0 0.3 convolution_multiply_fusion
  102.4 0.6 copy.33
  103.0 3.5 %all-to-all-done.4 = f32[8,1,128]{2,1,0:T(1,128)S(1)} async-done(((f32[8,1,128]{2,1,0:T(1,128)}), f32[8,1,128]{2,1,0:T(1,128)S(1)}, u32[]{:S(2)}, u32[]{:S(2)}) %all-to-all-start.4) | async-done | bytes 4128 | tf_op jit(solution)/shard_map/all_to_all | solution.py:40
  106.5 3.9 %all-to-all-start.2 = ((f32[8,8,5]{2,1,0:T(8,128)}), f32[8,8,5]{2,1,0:T(8,128)S(1)}, u32[]{:S(2)}, u32[]{:S(2)}) async-start(f32[8,8,5]{2,1,0:T(8,128)} %copy.33), calls=%async_computation.2 | async-start | bytes 65536 | tf_op jit(solution)/shard_map/all_to_all | solution.py:40
  110.5 0.6 reduce.4
  111.2 0.8 reshape.205
  112.0 3.2 %all-to-all-done.2 = f32[8,8,5]{2,1,0:T(8,128)S(1)} async-done(((f32[8,8,5]{2,1,0:T(8,128)}), f32[8,8,5]{2,1,0:T(8,128)S(1)}, u32[]{:S(2)}, u32[]{:S(2)}) %all-to-all-start.2) | async-done | bytes 1312 | tf_op jit(solution)/shard_map/all_to_all | solution.py:40
  115.2 6.2 %all-to-all-start.5 = ((f32[64,1,128]{2,1,0:T(1,128)}), f32[64,1,128]{2,1,0:T(1,128)S(1)}, u32[]{:S(2)}, u32[]{:S(2)}) async-start(f32[64,1,128]{2,1,0:T(1,128)} %reshape.205), calls=%async_computation.5 | async-start | bytes 65536 | tf_op jit(solution)/shard_map/all_to_all | solution.py:46
  121.4 0.6 reduce_sum.27
  122.0 12.7 %all-to-all-done.5 = f32[64,1,128]{2,1,0:T(1,128)S(1)} async-done(((f32[64,1,128]{2,1,0:T(1,128)}), f32[64,1,128]{2,1,0:T(1,128)S(1)}, u32[]{:S(2)}, u32[]{:S(2)}) %all-to-all-start.5) | async-done | bytes 32800 | tf_op jit(solution)/shard_map/all_to_all | solution.py:46
  134.7 0.7 reduce.5
  135.4 0.1 reshape.206
  135.6 0.8 reshape.141
  (33 shorter events, 1.0 us)
Async XLA Ops:
  0.6 33.2 %copy-start = (bf16[256,256]{1,0:T(8,128)(2,1)S(1)}, bf16[256,256]{1,0:T(8,128)(2,1)}, u32[]{:S(2)}) copy-start(bf16[256,256]{1,0:T(8,128)(2,1)} %param.11) | copy-start | bytes 393220
  0.6 25.2 %copy-start.1 = (bf16[8,40]{1,0:T(8,128)(2,1)S(1)}, bf16[8,40]{1,0:T(8,128)(2,1)}, u32[]{:S(2)}) copy-start(bf16[8,40]{1,0:T(8,128)(2,1)} %param.13) | copy-start | bytes 1924
  2.3 15.9 %collective-permute-start = (bf16[8,8,1024]{2,1,0:T(8,128)(2,1)S(1)}, bf16[8,8,1024]{2,1,0:T(8,128)(2,1)S(1)}, u32[]{:S(2)}, u32[]{:S(2)}) collective-permute-start(bf16[8,8,1024]{2,1,0:T(8,128)(2,1)S(1)} %broadcast_multiply_fusion), channel_id=1, source_target_pairs={{0,16},{8,24},{16,32},{24,40},{32,48},{40,56},{48,64},{56,72},{64,... | collective-permute-start | bytes 393224 | tf_op jit(solution)/shard_map/ppermute | solution.py:15
  8.1 10.2 %collective-permute-start.1 = (bf16[8,8,1024]{2,1,0:T(8,128)(2,1)S(1)}, bf16[8,8,1024]{2,1,0:T(8,128)(2,1)S(1)}, u32[]{:S(2)}, u32[]{:S(2)}) collective-permute-start(bf16[8,8,1024]{2,1,0:T(8,128)(2,1)S(1)} %broadcast_multiply_fusion), channel_id=1, source_target_pairs={{0,8},{8,16},{16,24},{24,32},{32,40},{40,48},{48,56},{56,64},{64,7... | collective-permute-start | bytes 393224 | tf_op jit(solution)/shard_map/ppermute | solution.py:15
  11.6 7.7 %collective-permute-start.2 = (bf16[8,8,1024]{2,1,0:T(8,128)(2,1)S(1)}, bf16[8,8,1024]{2,1,0:T(8,128)(2,1)S(1)}, u32[]{:S(2)}, u32[]{:S(2)}) collective-permute-start(bf16[8,8,1024]{2,1,0:T(8,128)(2,1)S(1)} %broadcast_multiply_fusion), channel_id=1, source_target_pairs={{8,0},{16,8},{24,16},{32,24},{40,32},{48,40},{56,48},{64,56},{72,6... | collective-permute-start | bytes 393224 | tf_op jit(solution)/shard_map/ppermute | solution.py:15
  12.9 12.5 %collective-permute-start.3 = (bf16[8,8,1024]{2,1,0:T(8,128)(2,1)S(1)}, bf16[8,8,1024]{2,1,0:T(8,128)(2,1)S(1)}, u32[]{:S(2)}, u32[]{:S(2)}) collective-permute-start(bf16[8,8,1024]{2,1,0:T(8,128)(2,1)S(1)} %broadcast_multiply_fusion), channel_id=1, source_target_pairs={{16,0},{24,8},{32,16},{40,24},{48,32},{56,40},{64,48},{72,56},{80,... | collective-permute-start | bytes 393224 | tf_op jit(solution)/shard_map/ppermute | solution.py:15
  26.8 13.5 %all-to-all-start = ((bf16[8,8,2048]{2,1,0:T(8,128)(2,1)}), bf16[8,8,2048]{2,1,0:T(8,128)(2,1)S(1)}, u32[]{:S(2)}, u32[]{:S(2)}) async-start(bf16[8,8,2048]{2,1,0:T(8,128)(2,1)} %pad_maximum_fusion), calls=%async_computation | async-start | bytes 524288 | tf_op jit(solution)/shard_map/all_to_all | solution.py:26
  40.3 2.1 %copy-start.2 = (bf16[256,256]{1,0:T(8,128)(2,1)S(1)}, bf16[256,256]{1,0:T(8,128)(2,1)}, u32[]{:S(2)}) copy-start(bf16[256,256]{1,0:T(8,128)(2,1)} %param.12) | copy-start | bytes 393220
  47.4 11.2 %all-to-all-start.1 = ((bf16[8,2,4096]{2,1,0:T(2,128)(2,1)}), bf16[8,2,4096]{2,1,0:T(2,128)(2,1)S(1)}, u32[]{:S(2)}, u32[]{:S(2)}) async-start(bf16[8,2,4096]{2,1,0:T(2,128)(2,1)} %reshape.199), calls=%async_computation.1 | async-start | bytes 262144 | tf_op jit(solution)/shard_map/all_to_all | solution.py:138
  58.6 34.4 %all-to-all-start.3 = ((f32[64,1,1024]{2,1,0:T(1,128)}), f32[64,1,1024]{2,1,0:T(1,128)S(1)}, u32[]{:S(2)}, u32[]{:S(2)}) async-start(f32[64,1,1024]{2,1,0:T(1,128)} %reshape.201), calls=%async_computation.3 | async-start | bytes 524288 | tf_op jit(solution)/shard_map/all_to_all | solution.py:40
  95.8 10.7 %all-to-all-start.4 = ((f32[8,1,128]{2,1,0:T(1,128)}), f32[8,1,128]{2,1,0:T(1,128)S(1)}, u32[]{:S(2)}, u32[]{:S(2)}) async-start(f32[8,1,128]{2,1,0:T(1,128)} %reshape.203), calls=%async_computation.4 | async-start | bytes 8192 | tf_op jit(solution)/shard_map/all_to_all | solution.py:40
  106.5 8.7 %all-to-all-start.2 = ((f32[8,8,5]{2,1,0:T(8,128)}), f32[8,8,5]{2,1,0:T(8,128)S(1)}, u32[]{:S(2)}, u32[]{:S(2)}) async-start(f32[8,8,5]{2,1,0:T(8,128)} %copy.33), calls=%async_computation.2 | async-start | bytes 65536 | tf_op jit(solution)/shard_map/all_to_all | solution.py:40
  115.2 19.5 %all-to-all-start.5 = ((f32[64,1,128]{2,1,0:T(1,128)}), f32[64,1,128]{2,1,0:T(1,128)S(1)}, u32[]{:S(2)}, u32[]{:S(2)}) async-start(f32[64,1,128]{2,1,0:T(1,128)} %reshape.205), calls=%async_computation.5 | async-start | bytes 65536 | tf_op jit(solution)/shard_map/all_to_all | solution.py:46
where the time goes:
time: 137 us; the launch traced here: 136 us
  starting transfers between devices  53.9 us (39%)
  waiting for transfers between devices  50.4 us (37%)
  local copies, waits for them, and re-layouts  15.2 us (11%)
  other arithmetic  12.3 us (9%)
  matrix products  3.47 us (3%)
    all_to_all x3, waiting for transfers between devices, summed_on_arrival(): lax.all_to_all(in_blocks(array, dim, peers), axis, 0, 0, tiled=True)  25.8 us
    all_to_all x3, starting transfers between devices, summed_on_arrival(): lax.all_to_all(in_blocks(array, dim, peers), axis, 0, 0, tiled=True)  24.6 us
    all_to_all x1, waiting for transfers between devices, from_everyone(): lax.all_to_all(jnp.broadcast_to(array[None], (peers, *array.shape)), axis...  12.7 us
    ppermute x4, starting transfers between devices, shifted(): lax.ppermute(value, axis, [(source, source + steps) for source in range(i...  11.9 us
    all_to_all x1, starting transfers between devices, side_by_side(): lax.all_to_all(both, axis, split_axis=split_dim, concat_axis=concat_dim,...  6.97 us
    all_to_all x1, starting transfers between devices, from_everyone(): lax.all_to_all(jnp.broadcast_to(array[None], (peers, *array.shape)), axis...  6.15 us
    ppermute x4, waiting for transfers between devices, shifted(): lax.ppermute(value, axis, [(source, source + steps) for source in range(i...  6.05 us
    all_to_all x1, waiting for transfers between devices, side_by_side(): lax.all_to_all(both, axis, split_axis=split_dim, concat_axis=concat_dim,...  5.85 us
  transfers between devices with their start and end apart: 10, of which 6 were waited for; matrix products, arithmetic and copies ran while one was open for 12% of the time, Pallas kernels for 0%

commit v1 on v0

--- a/solution.py
+++ b/solution.py
@@ -135,9 +135,11 @@
     sub_tiles, sub_mixed = side_by_side((masked, mixed_tiles), "pair", 0, 1, 2)
     orbital_form = tiles_to_matrix(sub_tiles, inverse)
     full_form = all_products(orbital_form, green_occ, green_vir)
-    products = lax.all_to_all(
-        matrix_to_tiles(full_form, pair_atoms), "pair", split_axis=1, concat_axis=0, tiled=True
-    )
+    x = matrix_to_tiles(full_form, pair_atoms)
+    n_dev = lax.axis_size("pair")
+    parts = jnp.stack(jnp.split(x, n_dev, axis=1), axis=0)
+    parts = lax.all_to_all(parts, "pair", split_axis=0, concat_axis=0)
+    products = jnp.concatenate(parts, axis=0)
     by_atom = energy_rows(
         sub_mixed, jnp.take(occ_rows, second_atom, axis=0), orbital_form, first_atom
     )

time: 137 us -> 139 us (1.015)
  local copies, waits for them, and re-layouts: 15.2 us -> 17.7 us
    unnamed x19 -> x24, local copies, waits for them, and re-layouts: 4.59 us -> 7.49 us
  transfers between devices with their start and end apart: 10 -> 10, of which waited for: 6 -> 6; matrix products, arithmetic and copies ran while one was open for 12% -> 11% of each run, Pallas kernels for 0% -> 0%
where the time goes in v1:
time: 139 us; the launch traced here: 138 us
  starting transfers between devices  53.8 us (39%)
  waiting for transfers between devices  51.3 us (37%)
  local copies, waits for them, and re-layouts  17.7 us (13%)
  other arithmetic  11 us (8%)
  matrix products  3.48 us (3%)
    all_to_all x3, waiting for transfers between devices, summed_on_arrival(): lax.all_to_all(in_blocks(array, dim, peers), axis, 0, 0, tiled=True)  26.7 us
    all_to_all x3, starting transfers between devices, summed_on_arrival(): lax.all_to_all(in_blocks(array, dim, peers), axis, 0, 0, tiled=True)  24.5 us
    all_to_all x1, waiting for transfers between devices, from_everyone(): lax.all_to_all(jnp.broadcast_to(array[None], (peers, *array.shape)), axis...  12.7 us
    ppermute x4, starting transfers between devices, shifted(): lax.ppermute(value, axis, [(source, source + steps) for source in range(i...  11.9 us
    unnamed x24, local copies, waits for them, and re-layouts  7.49 us
    all_to_all x1, starting transfers between devices, side_by_side(): lax.all_to_all(both, axis, split_axis=split_dim, concat_axis=concat_dim,...  6.97 us
    all_to_all x1, starting transfers between devices, from_everyone(): lax.all_to_all(jnp.broadcast_to(array[None], (peers, *array.shape)), axis...  6.15 us
    ppermute x4, waiting for transfers between devices, shifted(): lax.ppermute(value, axis, [(source, source + steps) for source in range(i...  6.04 us
  transfers between devices with their start and end apart: 10, of which 6 were waited for; matrix products, arithmetic and copies ran while one was open for 11% of the time, Pallas kernels for 0%

profile of v1, /device:TPU:1, one launch (start us, length us, event | category | flops | bytes accessed | tf_op | source)
XLA Modules:
  0.0 138.3 jit_solution(17545672671938203810)
XLA Ops:
  0.7 0.7 convert_bitcast_fusion
  1.4 1.0 broadcast_multiply_fusion
  2.3 5.7 %collective-permute-start = (bf16[8,8,1024]{2,1,0:T(8,128)(2,1)S(1)}, bf16[8,8,1024]{2,1,0:T(8,128)(2,1)S(1)}, u32[]{:S(2)}, u32[]{:S(2)}) collective-permute-start(bf16[8,8,1024]{2,1,0:T(8,128)(2,1)S(1)} %broadcast_multiply_fusion), channel_id=1, source_target_pairs={{0,16},{8,24},{16,32},{24,40},{32,48},{40,56},{48,64},{56,72},{64,... | collective-permute-start | bytes 393224 | tf_op jit(solution)/shard_map/ppermute | solution.py:15
  8.1 3.5 %collective-permute-start.1 = (bf16[8,8,1024]{2,1,0:T(8,128)(2,1)S(1)}, bf16[8,8,1024]{2,1,0:T(8,128)(2,1)S(1)}, u32[]{:S(2)}, u32[]{:S(2)}) collective-permute-start(bf16[8,8,1024]{2,1,0:T(8,128)(2,1)S(1)} %broadcast_multiply_fusion), channel_id=1, source_target_pairs={{0,8},{8,16},{16,24},{24,32},{32,40},{40,48},{48,56},{56,64},{64,7... | collective-permute-start | bytes 393224 | tf_op jit(solution)/shard_map/ppermute | solution.py:15
  11.6 1.3 collective-permute-start.2
  12.9 1.3 collective-permute-start.3
  14.2 0.7 and_select_fusion.1
  14.9 0.7 compare_and_fusion.2
  15.6 2.7 %sort.17 = (s32[64]{0:T(128)}, s32[64]{0:T(128)S(1)}) sort(s32[64]{0:T(128)} %param.10, s32[64]{0:T(128)S(1)} %iota.8), dimensions={0}, to_apply=%region_0.0 | sort | flops 384 | bytes 1024 | tf_op jit(solution)/shard_map/jit(argsort)/sort | solution.py:125
  18.3 1.0 constant_dynamic-update-slice_fusion.2
  19.4 6.0 %collective-permute-done.3 = bf16[8,8,1024]{2,1,0:T(8,128)(2,1)S(1)} collective-permute-done((bf16[8,8,1024]{2,1,0:T(8,128)(2,1)S(1)}, bf16[8,8,1024]{2,1,0:T(8,128)(2,1)S(1)}, u32[]{:S(2)}, u32[]{:S(2)}) %collective-permute-start.3) | collective-permute-done | bytes 131104 | tf_op jit(solution)/shard_map/ppermute | solution.py:15
  25.4 0.4 copy.39
  25.8 0.2 convolution_convert_fusion
  26.1 0.7 pad_maximum_fusion
  26.8 7.0 %all-to-all-start = ((bf16[8,8,2048]{2,1,0:T(8,128)(2,1)}), bf16[8,8,2048]{2,1,0:T(8,128)(2,1)S(1)}, u32[]{:S(2)}, u32[]{:S(2)}) async-start(bf16[8,8,2048]{2,1,0:T(8,128)(2,1)} %pad_maximum_fusion), calls=%async_computation | async-start | bytes 524288 | tf_op jit(solution)/shard_map/all_to_all | solution.py:26
  33.8 0.6 gather_fusion
  34.4 5.8 %all-to-all-done = bf16[8,8,2048]{2,1,0:T(8,128)(2,1)S(1)} async-done(((bf16[8,8,2048]{2,1,0:T(8,128)(2,1)}), bf16[8,8,2048]{2,1,0:T(8,128)(2,1)S(1)}, u32[]{:S(2)}, u32[]{:S(2)}) %all-to-all-start) | async-done | bytes 262176 | tf_op jit(solution)/shard_map/all_to_all | solution.py:26
  40.3 0.7 gather_fusion.2
  41.1 0.4 reshape.123
  41.5 0.2 copy.44
  41.7 0.4 reshape.124
  42.1 0.4 reshape.186
  42.4 0.5 convolution_convert_fusion.2
  42.9 0.2 reshape_reshape.10
  43.2 0.5 reshape.182
  43.8 0.7 gather_fusion.3
  44.6 0.6 constant_dynamic-update-slice_fusion.12
  45.2 0.6 constant_dynamic-update-slice_fusion.11
  45.8 0.6 constant_dynamic-update-slice_fusion.10
  46.4 0.6 constant_dynamic-update-slice_fusion.9
  47.0 0.6 constant_dynamic-update-slice_fusion.8
  47.6 0.6 constant_dynamic-update-slice_fusion.7
  48.2 0.6 constant_dynamic-update-slice_fusion.6
  48.8 0.6 constant_dynamic-update-slice_fusion.5
  49.4 4.3 %all-to-all-start.1 = ((bf16[8,1,8,1024]{3,2,1,0:T(8,128)(2,1)}), bf16[8,1,8,1024]{3,2,1,0:T(8,128)(2,1)S(1)}, u32[]{:S(2)}, u32[]{:S(2)}) async-start(bf16[8,1,8,1024]{3,2,1,0:T(8,128)(2,1)} %constant_dynamic-update-slice_fusion.5), calls=%async_computation.1 | async-start | bytes 262144 | tf_op jit(solution)/shard_map/all_to_all | solution.py:141
  53.7 0.2 copy.32
  53.9 0.8 copy.33
  54.6 0.5 fusion
  55.1 1.3 fusion.2
  56.4 0.8 fusion.8
  57.2 0.3 reshape_reshape.12
  57.5 0.6 copy.35
  58.1 0.5 reshape.162
  58.6 0.7 gather_fusion.1
  59.3 0.2 copy.36
  59.5 1.0 reshape.190
  60.5 14.2 %all-to-all-start.3 = ((f32[64,1,1024]{2,1,0:T(1,128)}), f32[64,1,1024]{2,1,0:T(1,128)S(1)}, u32[]{:S(2)}, u32[]{:S(2)}) async-start(f32[64,1,1024]{2,1,0:T(1,128)} %reshape.190), calls=%async_computation.3 | async-start | bytes 524288 | tf_op jit(solution)/shard_map/all_to_all | solution.py:40
  74.9 20.0 %all-to-all-done.3 = f32[64,1,1024]{2,1,0:T(1,128)S(1)} async-done(((f32[64,1,1024]{2,1,0:T(1,128)}), f32[64,1,1024]{2,1,0:T(1,128)S(1)}, u32[]{:S(2)}, u32[]{:S(2)}) %all-to-all-start.3) | async-done | bytes 262176 | tf_op jit(solution)/shard_map/all_to_all | solution.py:40
  94.9 0.5 broadcast.65
  95.4 1.3 reduce
  97.0 0.7 reshape.192
  97.7 6.3 %all-to-all-start.4 = ((f32[8,1,128]{2,1,0:T(1,128)}), f32[8,1,128]{2,1,0:T(1,128)S(1)}, u32[]{:S(2)}, u32[]{:S(2)}) async-start(f32[8,1,128]{2,1,0:T(1,128)} %reshape.192), calls=%async_computation.4 | async-start | bytes 8192 | tf_op jit(solution)/shard_map/all_to_all | solution.py:40
  104.0 0.3 convolution_multiply_fusion
  104.3 0.6 copy.31
  105.0 3.5 %all-to-all-done.4 = f32[8,1,128]{2,1,0:T(1,128)S(1)} async-done(((f32[8,1,128]{2,1,0:T(1,128)}), f32[8,1,128]{2,1,0:T(1,128)S(1)}, u32[]{:S(2)}, u32[]{:S(2)}) %all-to-all-start.4) | async-done | bytes 4128 | tf_op jit(solution)/shard_map/all_to_all | solution.py:40
  108.5 3.9 %all-to-all-start.2 = ((f32[8,8,5]{2,1,0:T(8,128)}), f32[8,8,5]{2,1,0:T(8,128)S(1)}, u32[]{:S(2)}, u32[]{:S(2)}) async-start(f32[8,8,5]{2,1,0:T(8,128)} %copy.31), calls=%async_computation.2 | async-start | bytes 65536 | tf_op jit(solution)/shard_map/all_to_all | solution.py:40
  112.4 0.6 reduce.1
  113.2 0.8 reshape.194
  113.9 3.2 %all-to-all-done.2 = f32[8,8,5]{2,1,0:T(8,128)S(1)} async-done(((f32[8,8,5]{2,1,0:T(8,128)}), f32[8,8,5]{2,1,0:T(8,128)S(1)}, u32[]{:S(2)}, u32[]{:S(2)}) %all-to-all-start.2) | async-done | bytes 1312 | tf_op jit(solution)/shard_map/all_to_all | solution.py:40
  117.2 6.1 %all-to-all-start.5 = ((f32[64,1,128]{2,1,0:T(1,128)}), f32[64,1,128]{2,1,0:T(1,128)S(1)}, u32[]{:S(2)}, u32[]{:S(2)}) async-start(f32[64,1,128]{2,1,0:T(1,128)} %reshape.194), calls=%async_computation.5 | async-start | bytes 65536 | tf_op jit(solution)/shard_map/all_to_all | solution.py:46
  123.3 0.6 reduce_sum.27
  123.9 12.7 %all-to-all-done.5 = f32[64,1,128]{2,1,0:T(1,128)S(1)} async-done(((f32[64,1,128]{2,1,0:T(1,128)}), f32[64,1,128]{2,1,0:T(1,128)S(1)}, u32[]{:S(2)}, u32[]{:S(2)}) %all-to-all-start.5) | async-done | bytes 32800 | tf_op jit(solution)/shard_map/all_to_all | solution.py:46
  136.6 0.7 reduce.2
  137.5 0.8 reshape.133
  (35 shorter events, 1.2 us)
Async XLA Ops:
  0.6 33.2 %copy-start = (bf16[256,256]{1,0:T(8,128)(2,1)S(1)}, bf16[256,256]{1,0:T(8,128)(2,1)}, u32[]{:S(2)}) copy-start(bf16[256,256]{1,0:T(8,128)(2,1)} %param.11) | copy-start | bytes 393220
  0.6 25.2 %copy-start.1 = (bf16[8,40]{1,0:T(8,128)(2,1)S(1)}, bf16[8,40]{1,0:T(8,128)(2,1)}, u32[]{:S(2)}) copy-start(bf16[8,40]{1,0:T(8,128)(2,1)} %param.13) | copy-start | bytes 1924
  2.3 15.9 %collective-permute-start = (bf16[8,8,1024]{2,1,0:T(8,128)(2,1)S(1)}, bf16[8,8,1024]{2,1,0:T(8,128)(2,1)S(1)}, u32[]{:S(2)}, u32[]{:S(2)}) collective-permute-start(bf16[8,8,1024]{2,1,0:T(8,128)(2,1)S(1)} %broadcast_multiply_fusion), channel_id=1, source_target_pairs={{0,16},{8,24},{16,32},{24,40},{32,48},{40,56},{48,64},{56,72},{64,... | collective-permute-start | bytes 393224 | tf_op jit(solution)/shard_map/ppermute | solution.py:15
  8.1 10.2 %collective-permute-start.1 = (bf16[8,8,1024]{2,1,0:T(8,128)(2,1)S(1)}, bf16[8,8,1024]{2,1,0:T(8,128)(2,1)S(1)}, u32[]{:S(2)}, u32[]{:S(2)}) collective-permute-start(bf16[8,8,1024]{2,1,0:T(8,128)(2,1)S(1)} %broadcast_multiply_fusion), channel_id=1, source_target_pairs={{0,8},{8,16},{16,24},{24,32},{32,40},{40,48},{48,56},{56,64},{64,7... | collective-permute-start | bytes 393224 | tf_op jit(solution)/shard_map/ppermute | solution.py:15
  11.6 7.7 %collective-permute-start.2 = (bf16[8,8,1024]{2,1,0:T(8,128)(2,1)S(1)}, bf16[8,8,1024]{2,1,0:T(8,128)(2,1)S(1)}, u32[]{:S(2)}, u32[]{:S(2)}) collective-permute-start(bf16[8,8,1024]{2,1,0:T(8,128)(2,1)S(1)} %broadcast_multiply_fusion), channel_id=1, source_target_pairs={{8,0},{16,8},{24,16},{32,24},{40,32},{48,40},{56,48},{64,56},{72,6... | collective-permute-start | bytes 393224 | tf_op jit(solution)/shard_map/ppermute | solution.py:15
  12.9 12.5 %collective-permute-start.3 = (bf16[8,8,1024]{2,1,0:T(8,128)(2,1)S(1)}, bf16[8,8,1024]{2,1,0:T(8,128)(2,1)S(1)}, u32[]{:S(2)}, u32[]{:S(2)}) collective-permute-start(bf16[8,8,1024]{2,1,0:T(8,128)(2,1)S(1)} %broadcast_multiply_fusion), channel_id=1, source_target_pairs={{16,0},{24,8},{32,16},{40,24},{48,32},{56,40},{64,48},{72,56},{80,... | collective-permute-start | bytes 393224 | tf_op jit(solution)/shard_map/ppermute | solution.py:15
  26.8 13.5 %all-to-all-start = ((bf16[8,8,2048]{2,1,0:T(8,128)(2,1)}), bf16[8,8,2048]{2,1,0:T(8,128)(2,1)S(1)}, u32[]{:S(2)}, u32[]{:S(2)}) async-start(bf16[8,8,2048]{2,1,0:T(8,128)(2,1)} %pad_maximum_fusion), calls=%async_computation | async-start | bytes 524288 | tf_op jit(solution)/shard_map/all_to_all | solution.py:26
  40.3 2.1 %copy-start.2 = (bf16[256,256]{1,0:T(8,128)(2,1)S(1)}, bf16[256,256]{1,0:T(8,128)(2,1)}, u32[]{:S(2)}) copy-start(bf16[256,256]{1,0:T(8,128)(2,1)} %param.12) | copy-start | bytes 393220
  49.4 11.2 %all-to-all-start.1 = ((bf16[8,1,8,1024]{3,2,1,0:T(8,128)(2,1)}), bf16[8,1,8,1024]{3,2,1,0:T(8,128)(2,1)S(1)}, u32[]{:S(2)}, u32[]{:S(2)}) async-start(bf16[8,1,8,1024]{3,2,1,0:T(8,128)(2,1)} %constant_dynamic-update-slice_fusion.5), calls=%async_computation.1 | async-start | bytes 262144 | tf_op jit(solution)/shard_map/all_to_all | solution.py:141
  60.5 34.3 %all-to-all-start.3 = ((f32[64,1,1024]{2,1,0:T(1,128)}), f32[64,1,1024]{2,1,0:T(1,128)S(1)}, u32[]{:S(2)}, u32[]{:S(2)}) async-start(f32[64,1,1024]{2,1,0:T(1,128)} %reshape.190), calls=%async_computation.3 | async-start | bytes 524288 | tf_op jit(solution)/shard_map/all_to_all | solution.py:40
  97.7 10.8 %all-to-all-start.4 = ((f32[8,1,128]{2,1,0:T(1,128)}), f32[8,1,128]{2,1,0:T(1,128)S(1)}, u32[]{:S(2)}, u32[]{:S(2)}) async-start(f32[8,1,128]{2,1,0:T(1,128)} %reshape.192), calls=%async_computation.4 | async-start | bytes 8192 | tf_op jit(solution)/shard_map/all_to_all | solution.py:40
  108.5 8.7 %all-to-all-start.2 = ((f32[8,8,5]{2,1,0:T(8,128)}), f32[8,8,5]{2,1,0:T(8,128)S(1)}, u32[]{:S(2)}, u32[]{:S(2)}) async-start(f32[8,8,5]{2,1,0:T(8,128)} %copy.31), calls=%async_computation.2 | async-start | bytes 65536 | tf_op jit(solution)/shard_map/all_to_all | solution.py:40
  117.2 19.5 %all-to-all-start.5 = ((f32[64,1,128]{2,1,0:T(1,128)}), f32[64,1,128]{2,1,0:T(1,128)S(1)}, u32[]{:S(2)}, u32[]{:S(2)}) async-start(f32[64,1,128]{2,1,0:T(1,128)} %reshape.194), calls=%async_computation.5 | async-start | bytes 65536 | tf_op jit(solution)/shard_map/all_to_all | solution.py:46
